TPU v7x, 32 devices: a whole 2x2x4 slice. The times are simulated.
32 devices in a mesh: expert: 8 (over z, x), dp: 4 (over y, core).
Axes of the slice: x: 2, y: 2, z: 4, core: 2. Of those that a mesh axis runs over, the one named last changes fastest.
Arguments:
- tokens: bfloat16 [1024, 3584], P('expert', 'dp'), may hold values from -6 to 6
- routes: int32 [1024, 2], P('expert'), may hold values from 0 to 3, all different within a row; in each aligned block of 128 rows (0 to 127, 128 to 255, ...) at most 96 rows name the same one
- logits: float32 [1024, 2], P('expert'), may hold values from -6 to 6
- cotangent: bfloat16 [1024, 3584], P('expert', 'dp'), may hold values from -6 to 6
- pair_flags: int32 [2], replicated, may hold values from -1000 to 999
- w_up: bfloat16 [3584, 4096], P('dp', 'expert'), may hold values from -0.09375 to 0.09375
- w_down: bfloat16 [3584, 4096], P('dp', 'expert'), may hold values from -0.1875 to 0.1875
Outputs:
- grad_tokens: bfloat16 [1024, 3584], P('expert', 'dp')
- grad_logits: float32 [1024, 2], P('expert')
- grad_up: bfloat16 [3584, 4096], P('dp', 'expert')
- grad_down: bfloat16 [3584, 4096], P('dp', 'expert')
Inputs may be any that keep to these rules, and one draw needn't show every extreme that they name: `routes`: among the 128 tokens of one index of the expert axis no expert is named more than 96 times, a bound that some block reaches; a token names 2 distinct experts.
All inputs are finite; a program needn't handle non-finite values.
Results may differ from a plain program's by a relative error of at most 0.02.
Values may be sent and summed in bfloat16 or wider, within the bound.
A program may use at most 64 MiB of HBM per device.

v0:
```python
import jax
import jax.numpy as jnp
from jax import lax
from jax.sharding import PartitionSpec as P


def passed_along(value, axis, steps):
    count = lax.axis_size(axis)
    pairs = [(source, (source + steps) % count) for source in range(count)]
    return lax.ppermute(value, axis, pairs)


def pick_pair(swapped_here, theirs, ours):
    return tuple(
        (
            jnp.where(swapped_here, other_part, mine_part)
            for other_part, mine_part in zip(theirs, ours)
        )
    )


def activate(up_pre, grad_hidden):
    up_sig = jax.nn.sigmoid(up_pre)
    hidden = (up_pre * up_sig).astype(jnp.bfloat16)
    pairing_part = jnp.sum(hidden.astype(jnp.float32) * grad_hidden, -1)
    grad_pre = (grad_hidden * up_sig * (1.0 + up_pre * (1.0 - up_sig))).astype(jnp.bfloat16)
    return (hidden, pairing_part, grad_pre)


def local(tokens, routes, logits, cotangent, pair_flags, w_up, w_down):
    devices_ex = lax.axis_size("expert")
    experts = devices_ex // 2
    half_way = experts // 2
    here_index = lax.axis_index("expert")
    slot_here = here_index // 2
    tok_rows, top_count = routes.shape
    quarter = tokens.shape[1]
    capacity = max(2, 2 * (3 * tok_rows * top_count // (4 * experts)))
    expert_ids = jnp.arange(experts, dtype=jnp.int32)
    paired = jnp.concatenate([pair_flags, pair_flags]) > 0
    owner_slot = jnp.where(paired, (expert_ids + half_way) % experts, expert_ids)
    swapped_here = paired[slot_here]
    affinity = jax.nn.sigmoid(logits)
    weights = affinity / jnp.sum(affinity, -1, keepdims=True)
    scaled = (weights[:, :, None] * cotangent[:, None, :].astype(jnp.float32)).astype(jnp.bfloat16)
    scaled = scaled.reshape(-1, quarter)
    flat_routes = routes.reshape(-1)
    onehot = (flat_routes[:, None] == expert_ids[None, :]).astype(jnp.int32)
    slot_rank = jnp.sum(jnp.cumsum(onehot, 0) * onehot, 1) - 1
    own_weights = (w_up, w_down)
    shifted = passed_along((w_up, w_down), "expert", devices_ex // 2)
    resident = pick_pair(swapped_here, shifted, own_weights)
    target = owner_slot[flat_routes]
    position = target * capacity + slot_rank
    empty_rows = jnp.zeros((experts * capacity, quarter), jnp.bfloat16)
    token_buf = (
        empty_rows.at[position]
        .set(jnp.repeat(tokens, top_count, axis=0))
        .reshape(experts, capacity, quarter)
    )
    scaled_buf = empty_rows.at[position].set(scaled).reshape(experts, capacity, quarter)
    token_in, scaled_in = (
        lax.all_to_all(
            jnp.repeat(token_buf, 2, axis=0), "expert", split_axis=0, concat_axis=0, tiled=True
        ),
        lax.all_to_all(
            jnp.repeat(scaled_buf, 2, axis=0), "expert", split_axis=0, concat_axis=0, tiled=True
        ),
    )
    routed_rows = token_in.reshape(-1, quarter)
    scaled_rows = scaled_in.reshape(-1, quarter)
    up_block, down_block = resident
    up_part = jnp.dot(routed_rows, up_block, preferred_element_type=jnp.float32)
    grad_part = jnp.dot(scaled_rows, down_block, preferred_element_type=jnp.float32)
    up_pre, grad_hidden = (
        lax.psum(up_part.astype(jnp.bfloat16), "dp").astype(jnp.float32),
        lax.psum(grad_part.astype(jnp.bfloat16), "dp").astype(jnp.float32),
    )
    hidden, pairing_part, grad_pre = activate(up_pre, grad_hidden)
    pairing_half = pairing_part.astype(jnp.bfloat16)
    route_half = jnp.einsum(
        "nf,df->nd", grad_pre, up_block, preferred_element_type=jnp.float32
    ).astype(jnp.bfloat16)
    grad_up = jnp.einsum(
        "nd,nf->df", routed_rows, grad_pre, preferred_element_type=jnp.float32
    ).astype(jnp.bfloat16)
    grad_down = jnp.einsum(
        "nd,nf->df", scaled_rows, hidden, preferred_element_type=jnp.float32
    ).astype(jnp.bfloat16)
    back_rows, back_pairing = (
        lax.all_to_all(
            route_half.reshape(devices_ex, capacity, quarter),
            "expert",
            split_axis=0,
            concat_axis=0,
            tiled=True,
        ),
        lax.all_to_all(
            pairing_half.reshape(devices_ex, capacity),
            "expert",
            split_axis=0,
            concat_axis=0,
            tiled=True,
        ),
    )
    back_grid = back_rows.reshape(experts, 2, capacity, quarter)
    picked = back_grid[target, :, slot_rank]
    grad_tokens = jnp.sum(
        picked.astype(jnp.float32).reshape(tok_rows, top_count * 2, quarter), 1
    ).astype(jnp.bfloat16)
    pair_grid = back_pairing.reshape(experts, 2, capacity)
    pair_picked = pair_grid[target, :, slot_rank]
    pairing_mine = jnp.sum(pair_picked.astype(jnp.float32), 1).reshape(tok_rows, top_count)
    grad_logits = (1.0 - affinity) * (
        pairing_mine - weights * jnp.sum(pairing_mine, -1, keepdims=True)
    )
    return (grad_tokens, grad_logits, grad_up, grad_down)


def solution(mesh):
    in_specs = (
        P("expert", "dp"),
        P("expert", None),
        P("expert", None),
        P("expert", "dp"),
        P(),
        P("dp", "expert"),
        P("dp", "expert"),
    )
    out_specs = (P("expert", "dp"), P("expert", None), P("dp", "expert"), P("dp", "expert"))
    return jax.shard_map(local, mesh=mesh, in_specs=in_specs, out_specs=out_specs, check_vma=False)
```

profile of v0, /device:TPU:0, one launch (start us, length us, event | category | flops | bytes accessed | tf_op | source)
XLA Modules:
  0.0 291.5 jit_solution(14020023597127214736)
XLA Ops:
  11.4 2.6 fusion.21
  17.0 1.9 scatter_custom_fusion
  20.1 7.4 %all-to-all-start = ((bf16[8,96,896]{2,1,0:T(8,128)(2,1)}), bf16[8,96,896]{2,1,0:T(8,128)(2,1)S(1)}, u32[]{:S(2)}, u32[]{:S(2)}) async-start(bf16[8,96,896]{2,1,0:T(8,128)(2,1)} %bitcast.9), calls=%async_computation | async-start | bytes 2752512 | tf_op jit(solution)/shard_map/all_to_all | solution.py:66
  28.0 1.9 scatter_custom_fusion.1
  29.8 30.5 %all-to-all-done = bf16[8,96,896]{2,1,0:T(8,128)(2,1)S(1)} async-done(((bf16[8,96,896]{2,1,0:T(8,128)(2,1)}), bf16[8,96,896]{2,1,0:T(8,128)(2,1)S(1)}, u32[]{:S(2)}, u32[]{:S(2)}) %all-to-all-start) | async-done | bytes 1376288 | tf_op jit(solution)/shard_map/all_to_all | solution.py:66
  61.5 3.6 %all-to-all-start.1 = ((bf16[8,96,896]{2,1,0:T(8,128)(2,1)}), bf16[8,96,896]{2,1,0:T(8,128)(2,1)S(1)}, u32[]{:S(2)}, u32[]{:S(2)}) async-start(bf16[8,96,896]{2,1,0:T(8,128)(2,1)} %bitcast.13), calls=%async_computation.1 | async-start | bytes 2752512 | tf_op jit(solution)/shard_map/all_to_all | solution.py:63
  65.2 2.9 collective-permute-start
  68.8 89.7 %collective-permute-done = bf16[896,512]{1,0:T(8,128)(2,1)} collective-permute-done((bf16[896,512]{1,0:T(8,128)(2,1)}, bf16[896,512]{1,0:T(8,128)(2,1)}, u32[]{:S(2)}, u32[]{:S(2)}) %collective-permute-start) | collective-permute-done | bytes 917536 | tf_op jit(solution)/shard_map/ppermute | solution.py:10
  158.4 3.7 %convolution_convert_fusion.4 = bf16[768,512]{1,0:T(8,128)(2,1)} fusion(bf16[768,896]{1,0:T(8,128)(2,1)S(1)} %bitcast.44, bf16[896,512]{1,0:T(8,128)(2,1)} %collective-permute-done, bf16[896,512]{1,0:T(8,128)(2,1)} %param.13, pred[]{:T(512)} %bitcast.11), kind=kOutput, calls=%fused_computation.22 | convolution fusion | flops 705495040 | bytes 3997697 | tf_op jit(solution)/shard_map/dot_general | solution.py:74
  162.2 14.7 %collective-permute-done.1 = bf16[896,512]{1,0:T(8,128)(2,1)} collective-permute-done((bf16[896,512]{1,0:T(8,128)(2,1)}, bf16[896,512]{1,0:T(8,128)(2,1)}, u32[]{:S(2)}, u32[]{:S(2)}) %collective-permute-start.1) | collective-permute-done | bytes 917536 | tf_op jit(solution)/shard_map/ppermute | solution.py:10
  176.9 3.7 %convolution_convert_fusion.3 = bf16[768,512]{1,0:T(8,128)(2,1)} fusion(bf16[768,896]{1,0:T(8,128)(2,1)S(1)} %bitcast.46, bf16[896,512]{1,0:T(8,128)(2,1)} %collective-permute-done.1, bf16[896,512]{1,0:T(8,128)(2,1)} %param.12, pred[]{:T(512)} %bitcast.11), kind=kOutput, calls=%fused_computation.21 | convolution fusion | flops 705495040 | bytes 3997697 | tf_op jit(solution)/shard_map/dot_general | solution.py:73
  180.6 42.3 %all-reduce.3.cloned.1.call-done = (bf16[768,512]{1,0:T(8,128)(2,1)}, bf16[768,512]{1,0:T(8,128)(2,1)}) async-done(((bf16[768,512]{1,0:T(8,128)(2,1)}, bf16[768,512]{1,0:T(8,128)(2,1)}), (bf16[768,512]{1,0:T(8,128)(2,1)}, bf16[768,512]{1,0:T(8,128)(2,1)})) %all-reduce.3.cloned.1.call-update) | async-done | bytes 1572880 | tf_op jit(solution)/shard_map/psum | solution.py:77
  222.9 2.0 fusion.2
  225.7 5.5 %all-to-all-start.3 = ((bf16[8,1,96]{2,1,0:T(2,128)(2,1)}), bf16[8,1,96]{2,1,0:T(2,128)(2,1)S(1)}, u32[]{:S(2)}, u32[]{:S(2)}) async-start(bf16[8,1,96]{2,1,0:T(2,128)(2,1)} %convert_element_type.86), calls=%async_computation.3 | async-start | bytes 8192 | tf_op jit(solution)/shard_map/all_to_all | solution.py:98
  231.2 4.3 %convolution_convert_fusion = bf16[768,896]{1,0:T(8,128)(2,1)} fusion(bf16[896,512]{1,0:T(8,128)(2,1)} %collective-permute-done.1, bf16[896,512]{1,0:T(8,128)(2,1)} %param.12, pred[]{:T(512)} %bitcast.11, bf16[768,512]{1,0:T(8,128)(2,1)S(1)} %copy-done.2, bf16[768,512]{1,0:T(8,128)(2,1)S(1)} %copy-done.4), kind=kOutput, calls=%fused_computation.10 | convolution fusion | flops 710115328 | bytes 4784129 | tf_op jit(solution)/shard_map/nf,df->nd/dot_general | solution.py:81
  235.5 2.1 all-to-all-done.3
  237.6 3.9 %all-to-all-start.2 = ((bf16[8,96,896]{2,1,0:T(8,128)(2,1)}), bf16[8,96,896]{2,1,0:T(8,128)(2,1)S(1)}, u32[]{:S(2)}, u32[]{:S(2)}) async-start(bf16[8,96,896]{2,1,0:T(8,128)(2,1)} %bitcast.48), calls=%async_computation.2 | async-start | bytes 2752512 | tf_op jit(solution)/shard_map/all_to_all | solution.py:91
  241.5 3.2 %convolution_convert_fusion.1 = bf16[896,512]{1,0:T(8,128)(2,1)} fusion(bf16[768,896]{1,0:T(8,128)(2,1)S(1)} %bitcast.45, bf16[768,512]{1,0:T(8,128)(2,1)} %get-tuple-element.25), kind=kOutput, calls=%fused_computation.19 | convolution fusion | flops 707461120 | bytes 3080192 | tf_op jit(solution)/shard_map/nd,nf->df/dot_general | solution.py:87
  244.7 2.0 convolution_convert_fusion.2
  246.9 1.7 gather_fusion.1
  249.7 24.0 %all-to-all-done.2 = bf16[8,96,896]{2,1,0:T(8,128)(2,1)S(1)} async-done(((bf16[8,96,896]{2,1,0:T(8,128)(2,1)}), bf16[8,96,896]{2,1,0:T(8,128)(2,1)S(1)}, u32[]{:S(2)}, u32[]{:S(2)}) %all-to-all-start.2) | async-done | bytes 1376288 | tf_op jit(solution)/shard_map/all_to_all | solution.py:91
  274.7 3.7 %gather_fusion = bf16[256,2,896]{2,1,0:T(2,128)(2,1)} fusion(bf16[4,2,96,896]{3,1,2,0:T(2,128)(2,1)S(1)} %copy.56, s32[256]{0:T(256)S(1)} %bitcast.40), kind=kCustom, calls=%fused_computation | custom fusion | bytes 1837056 | tf_op jit(solution)/shard_map/gather | solution.py:107
  278.4 3.8 %convert_reduce_fusion = f32[256,896]{1,0:T(8,128)S(1)} fusion(bf16[256,2,896]{2,1,0:T(2,128)(2,1)} %gather_fusion), kind=kLoop, calls=%fused_computation.9 | loop fusion | flops 688128 | bytes 1835008 | tf_op jit(solution)/shard_map/reduce_sum | solution.py:108
  282.8 1.9 reduce_sum.65
  (56 shorter events, 14.3 us)
Async XLA Ops:
  20.1 7.4 %copy-start.6 = (bf16[128,896]{1,0:T(8,128)(2,1)S(1)}, bf16[128,896]{1,0:T(8,128)(2,1)}, u32[]{:S(2)}) copy-start(bf16[128,896]{1,0:T(8,128)(2,1)} %param.7) | copy-start | bytes 688132
  20.1 40.2 %all-to-all-start = ((bf16[8,96,896]{2,1,0:T(8,128)(2,1)}), bf16[8,96,896]{2,1,0:T(8,128)(2,1)S(1)}, u32[]{:S(2)}, u32[]{:S(2)}) async-start(bf16[8,96,896]{2,1,0:T(8,128)(2,1)} %bitcast.9), calls=%async_computation | async-start | bytes 2752512 | tf_op jit(solution)/shard_map/all_to_all | solution.py:66
  61.5 115.4 %all-to-all-start.1 = ((bf16[8,96,896]{2,1,0:T(8,128)(2,1)}), bf16[8,96,896]{2,1,0:T(8,128)(2,1)S(1)}, u32[]{:S(2)}, u32[]{:S(2)}) async-start(bf16[8,96,896]{2,1,0:T(8,128)(2,1)} %bitcast.13), calls=%async_computation.1 | async-start | bytes 2752512 | tf_op jit(solution)/shard_map/all_to_all | solution.py:63
  65.2 157.8 %all-reduce.3.cloned.1.call-start = ((), (), s32[]{:S(2)}) async-start(), calls=%async_computation.4 | async-start | bytes 3145728 | tf_op jit(solution)/shard_map/psum | solution.py:77
  65.2 93.2 %collective-permute-start = (bf16[896,512]{1,0:T(8,128)(2,1)}, bf16[896,512]{1,0:T(8,128)(2,1)}, u32[]{:S(2)}, u32[]{:S(2)}) collective-permute-start(bf16[896,512]{1,0:T(8,128)(2,1)} %param.13), channel_id=1, source_target_pairs={{0,16},{4,20},{8,24},{12,28},{16,0},{20,4},{24,8},{28,12},{1,17},{... | collective-permute-start | bytes 2752520 | tf_op jit(solution)/shard_map/ppermute | solution.py:10
  68.1 108.8 %collective-permute-start.1 = (bf16[896,512]{1,0:T(8,128)(2,1)}, bf16[896,512]{1,0:T(8,128)(2,1)}, u32[]{:S(2)}, u32[]{:S(2)}) collective-permute-start(bf16[896,512]{1,0:T(8,128)(2,1)} %param.12), channel_id=1, source_target_pairs={{0,16},{4,20},{8,24},{12,28},{16,0},{20,4},{24,8},{28,12},{1,17},{... | collective-permute-start | bytes 2752520 | tf_op jit(solution)/shard_map/ppermute | solution.py:10
  176.9 3.7 %copy-start = (bf16[8,96,896]{2,1,0:T(8,128)(2,1)}, bf16[8,96,896]{2,1,0:T(8,128)(2,1)S(1)}, u32[]{:S(2)}) copy-start(bf16[8,96,896]{2,1,0:T(8,128)(2,1)S(1)} %all-to-all-done.1) | copy-start | bytes 4128772
  222.9 8.2 %copy-start.2 = (bf16[768,512]{1,0:T(8,128)(2,1)S(1)}, bf16[768,512]{1,0:T(8,128)(2,1)}, u32[]{:S(2)}) copy-start(bf16[768,512]{1,0:T(8,128)(2,1)} %get-tuple-element.24) | copy-start | bytes 2359300
  222.9 8.2 %copy-start.4 = (bf16[768,512]{1,0:T(8,128)(2,1)S(1)}, bf16[768,512]{1,0:T(8,128)(2,1)}, u32[]{:S(2)}) copy-start(bf16[768,512]{1,0:T(8,128)(2,1)} %get-tuple-element.25) | copy-start | bytes 2359300
  225.7 11.9 %all-to-all-start.3 = ((bf16[8,1,96]{2,1,0:T(2,128)(2,1)}), bf16[8,1,96]{2,1,0:T(2,128)(2,1)S(1)}, u32[]{:S(2)}, u32[]{:S(2)}) async-start(bf16[8,1,96]{2,1,0:T(2,128)(2,1)} %convert_element_type.86), calls=%async_computation.3 | async-start | bytes 8192 | tf_op jit(solution)/shard_map/all_to_all | solution.py:98
  237.6 36.1 %all-to-all-start.2 = ((bf16[8,96,896]{2,1,0:T(8,128)(2,1)}), bf16[8,96,896]{2,1,0:T(8,128)(2,1)S(1)}, u32[]{:S(2)}, u32[]{:S(2)}) async-start(bf16[8,96,896]{2,1,0:T(8,128)(2,1)} %bitcast.48), calls=%async_computation.2 | async-start | bytes 2752512 | tf_op jit(solution)/shard_map/all_to_all | solution.py:91
  241.4 3.3 %copy-start.1 = (bf16[8,96,896]{2,1,0:T(8,128)(2,1)S(1)}, bf16[8,96,896]{2,1,0:T(8,128)(2,1)}, u32[]{:S(2)}) copy-start(bf16[8,96,896]{2,1,0:T(8,128)(2,1)} %copy-done) | copy-start | bytes 4128772
  241.4 3.3 %copy-start.3 = (bf16[768,512]{1,0:T(8,128)(2,1)S(1)}, bf16[768,512]{1,0:T(8,128)(2,1)}, u32[]{:S(2)}) copy-start(bf16[768,512]{1,0:T(8,128)(2,1)} %get-tuple-element.24) | copy-start | bytes 2359300
  241.5 3.2 %copy-start.5 = (bf16[768,512]{1,0:T(8,128)(2,1)S(1)}, bf16[768,512]{1,0:T(8,128)(2,1)}, u32[]{:S(2)}) copy-start(bf16[768,512]{1,0:T(8,128)(2,1)} %get-tuple-element.25) | copy-start | bytes 2359300
Sparse Core Ops, SparseCore 0:
  180.8 42.1 all-reduce.2
where the time goes:
time: 292 us
  waiting for transfers between devices  203 us (70%)
  starting transfers between devices  23.4 us (8%)
  local copies, waits for them, and re-layouts  18.6 us (6%)
  matrix products  17 us (6%)
  other arithmetic  15 us (5%)
  between operations  14.2 us (5%)
    ppermute x2, waiting for transfers between devices, passed_along(): return lax.ppermute(value, axis, pairs)  104 us
    psum x1, waiting for transfers between devices, local(): lax.psum(grad_part.astype(jnp.bfloat16), 'dp').astype(jnp.float32)  42.3 us
    all_to_all x1, waiting for transfers between devices, local(): lax.all_to_all(jnp.repeat(scaled_buf, 2, axis=0), 'expert', split_axis=0,...  30.5 us
    all_to_all x1, waiting for transfers between devices, local(): lax.all_to_all(route_half.reshape(devices_ex, capacity, quarter), 'expert...  24 us
    all_to_all x1, starting transfers between devices, local(): lax.all_to_all(jnp.repeat(scaled_buf, 2, axis=0), 'expert', split_axis=0,...  7.38 us
  transfers between devices with their start and end apart: 7, of which 6 were waited for; matrix products, arithmetic and copies ran while one was open for 7% of the time, Pallas kernels for 0%

commit v1 on v0

--- a/solution.py
+++ b/solution.py
@@ -116,6 +116,53 @@
     )
     return (grad_tokens, grad_logits, grad_up, grad_down)
 
+def dense(tokens, routes, logits, cotangent, pair_flags, w_up, w_down):
+    devices_ex = lax.axis_size("expert")
+    experts = devices_ex // 2
+    half_way = experts // 2
+    here_index = lax.axis_index("expert")
+    dp_count = lax.axis_size("dp")
+    slot_here = here_index // 2
+    tok_rows, top_count = routes.shape
+    expert_ids = jnp.arange(experts, dtype=jnp.int32)
+    paired = jnp.concatenate([pair_flags, pair_flags]) > 0
+    swapped_here = paired[slot_here]
+    owner_here = jnp.where(swapped_here, (slot_here + half_way) % experts, slot_here)
+    affinity = jax.nn.sigmoid(logits)
+    weights = affinity / jnp.sum(affinity, -1, keepdims=True)
+    chosen = (routes[:, :, None] == expert_ids[None, None, :]).astype(jnp.float32)
+    spread = jnp.sum(weights[:, :, None] * chosen, 1)
+    spread_all = lax.all_gather(spread, "expert", axis=0, tiled=True)
+    tokens_all = lax.all_gather(tokens, "expert", axis=0, tiled=True)
+    cot_all = lax.all_gather(cotangent, "expert", axis=0, tiled=True)
+    cot_wide = cot_all.astype(jnp.float32)
+    scaled_home = (lax.dynamic_slice_in_dim(spread_all, slot_here, 1, 1) * cot_wide).astype(jnp.bfloat16)
+    scaled_slot = (lax.dynamic_slice_in_dim(spread_all, owner_here, 1, 1) * cot_wide).astype(jnp.bfloat16)
+    up_part = jnp.dot(tokens_all, w_up, preferred_element_type=jnp.float32).astype(jnp.bfloat16)
+    grad_part = jnp.dot(scaled_home, w_down, preferred_element_type=jnp.float32).astype(jnp.bfloat16)
+    both = lax.psum_scatter(jnp.concatenate([up_part, grad_part], 1), "dp", scatter_dimension=0, tiled=True)
+    up_pre, grad_hidden = jnp.split(both.astype(jnp.float32), 2, axis=1)
+    hidden, pairing_part, grad_pre = activate(up_pre, grad_hidden)
+    pair_all = lax.all_gather(
+        pairing_part.astype(jnp.bfloat16)[None], ("expert", "dp"), axis=0, tiled=True
+    )
+    joined = jnp.concatenate([grad_pre, hidden], 1)
+    theirs = passed_along(joined, "expert", devices_ex // 2)
+    slot_joined = jnp.where(swapped_here, theirs, joined)
+    gathered = lax.all_gather(jnp.concatenate([grad_pre, slot_joined], 1), "dp", axis=0, tiled=True)
+    grad_home, grad_slot, hidden_slot = jnp.split(gathered, 3, axis=1)
+    route_part = jnp.einsum("nf,df->nd", grad_home, w_up, preferred_element_type=jnp.float32).astype(jnp.bfloat16)
+    grad_up = jnp.einsum("nd,nf->df", tokens_all, grad_slot, preferred_element_type=jnp.float32).astype(jnp.bfloat16)
+    grad_down = jnp.einsum("nd,nf->df", scaled_slot, hidden_slot, preferred_element_type=jnp.float32).astype(jnp.bfloat16)
+    grad_tokens = lax.psum_scatter(route_part, "expert", scatter_dimension=0, tiled=True)
+    pair_grid = pair_all.reshape(experts, 2, devices_ex, tok_rows)
+    pair_mine = jnp.sum(pair_grid[:, :, here_index].astype(jnp.float32), 1)
+    pairing_mine = jnp.sum(chosen * pair_mine.T[:, None, :], -1)
+    grad_logits = (1.0 - affinity) * (
+        pairing_mine - weights * jnp.sum(pairing_mine, -1, keepdims=True)
+    )
+    return (grad_tokens, grad_logits, grad_up, grad_down)
+
 
 def solution(mesh):
     in_specs = (
@@ -127,5 +174,6 @@
         P("dp", "expert"),
         P("dp", "expert"),
     )
+    body = dense if mesh.shape["expert"] <= 8 else local
     out_specs = (P("expert", "dp"), P("expert", None), P("dp", "expert"), P("dp", "expert"))
-    return jax.shard_map(local, mesh=mesh, in_specs=in_specs, out_specs=out_specs, check_vma=False)
+    return jax.shard_map(body, mesh=mesh, in_specs=in_specs, out_specs=out_specs, check_vma=False)

time: 292 us -> 278 us (0.952)
  blocking collectives: 0 us -> 68.5 us
  waiting for transfers between devices: 203 us -> 164 us
  starting transfers between devices: 23.4 us -> 2.69 us
  local copies, waits for them, and re-layouts: 18.6 us -> 1.93 us
  other arithmetic: 15 us -> 8.27 us
    all_gather x0 -> x3, waiting for transfers between devices: none -> 92 us  [the longest x1 44.7 us: dense(): cot_all = lax.all_gather(cotangent, 'expert', axis=0, tiled=True)]
    ppermute x2 -> x1, waiting for transfers between devices: 104 us -> 23.4 us  [passed_along(): return lax.ppermute(value, axis, pairs)]
    all_gather x0 -> x2, blocking collectives: none -> 68.5 us  [the longest x1 40.6 us: dense(): lax.all_gather(pairing_part.astype(jnp.bfloat16)[None], ('expert', 'dp'),...]
    all_to_all x4 -> x0, waiting for transfers between devices: 56.6 us -> none  [the longest x1 30.5 us: local(): lax.all_to_all(jnp.repeat(scaled_buf, 2, axis=0), 'expert', split_axis=0,...]
    reduce_scatter x0 -> x2, waiting for transfers between devices: none -> 47.6 us  [the longest x1 30.6 us: dense(): lax.psum_scatter(jnp.concatenate([up_part, grad_part], 1), 'dp', scatter_...]
    psum x1 -> x0, waiting for transfers between devices: 42.3 us -> none  [local(): lax.psum(grad_part.astype(jnp.bfloat16), 'dp').astype(jnp.float32)]
    all_to_all x4 -> x0, starting transfers between devices: 20.4 us -> none  [the longest x1 7.38 us: local(): lax.all_to_all(jnp.repeat(scaled_buf, 2, axis=0), 'expert', split_axis=0,...]
    gather x3 -> x0, local copies, waits for them, and re-layouts: 5.93 us -> none  [the longest x1 3.67 us: local(): picked = back_grid[target, :, slot_rank]]
  transfers between devices with their start and end apart: 7 -> 6, of which waited for: 6 -> 6; matrix products, arithmetic and copies ran while one was open for 7% -> 6% of each run, Pallas kernels for 0% -> 0%
where the time goes in v1:
time: 278 us; the launch traced here: 277 us
  waiting for transfers between devices  164 us (59%)
  blocking collectives  68.5 us (25%)
  matrix products  16.7 us (6%)
  between operations  14.6 us (5%)
  other arithmetic  8.27 us (3%)
    all_gather x1, waiting for transfers between devices, dense(): cot_all = lax.all_gather(cotangent, 'expert', axis=0, tiled=True)  44.7 us
    all_gather x1, blocking collectives, dense(): lax.all_gather(pairing_part.astype(jnp.bfloat16)[None], ('expert', 'dp'),...  40.6 us
    reduce_scatter x1, waiting for transfers between devices, dense(): lax.psum_scatter(jnp.concatenate([up_part, grad_part], 1), 'dp', scatter_...  30.6 us
    all_gather x1, waiting for transfers between devices, dense(): lax.all_gather(jnp.concatenate([grad_pre, slot_joined], 1), 'dp', axis=0,...  29 us
    all_gather x1, blocking collectives, dense(): spread_all = lax.all_gather(spread, 'expert', axis=0, tiled=True)  27.9 us
    ppermute x1, waiting for transfers between devices, passed_along(): return lax.ppermute(value, axis, pairs)  23.4 us
    all_gather x1, waiting for transfers between devices, dense(): tokens_all = lax.all_gather(tokens, 'expert', axis=0, tiled=True)  18.3 us
    reduce_scatter x1, waiting for transfers between devices, dense(): lax.psum_scatter(route_part, 'expert', scatter_dimension=0, tiled=True)  17 us
  transfers between devices with their start and end apart: 6, of which 6 were waited for; matrix products, arithmetic and copies ran while one was open for 6% of the time, Pallas kernels for 0%

profile of v1, /device:TPU:0, one launch (start us, length us, event | category | flops | bytes accessed | tf_op | source)
XLA Modules:
  0.0 277.1 jit_solution(8674102475875058742)
XLA Ops:
  8.0 0.7 all-gather.8.cloned.1.call-update
  8.7 0.8 add_compare_fusion
  10.8 0.7 fusion.18
  11.5 0.7 multiply_divide_fusion
  12.2 0.7 select_reduce_fusion.2
  12.9 27.9 %all_gather.16 = f32[1024,4]{0,1:T(4,128)S(1)} all-gather(f32[128,4]{0,1:T(4,128)S(1)} %select_reduce_fusion.2), channel_id=1, replica_groups=mesh['expert'=8,'dp'=4] {'expert'}, dimensions={0}, use_global_device_ids=true | all-gather | bytes 18432 | tf_op jit(solution)/shard_map/all_gather | solution.py:135
  40.8 18.3 %all-gather.6.cloned.1.call-done = bf16[1024,896]{1,0:T(8,128)(2,1)} async-done(((bf16[128,896]{1,0:T(8,128)(2,1)}), bf16[1024,896]{1,0:T(8,128)(2,1)}) %all-gather.6.cloned.1.call-update) | async-done | bytes 1835024 | tf_op jit(solution)/shard_map/all_gather | solution.py:136
  59.2 2.8 %convolution_convert_fusion.1 = bf16[1024,512]{0,1:T(8,128)(2,1)S(1)} fusion(bf16[1024,896]{1,0:T(8,128)(2,1)} %all-gather.6.cloned.1.call-done, bf16[896,512]{1,0:T(8,128)(2,1)S(1)} %copy-done), kind=kOutput, calls=%fused_computation.11 | convolution fusion | flops 940048384 | bytes 3801088 | tf_op jit(solution)/shard_map/dot_general | solution.py:141
  62.0 44.7 %all-gather.8.cloned.1.call-done = bf16[1024,896]{1,0:T(8,128)(2,1)} async-done(((bf16[128,896]{1,0:T(8,128)(2,1)}), bf16[1024,896]{1,0:T(8,128)(2,1)}) %all-gather.8.cloned.1.call-update) | async-done | bytes 1835024 | tf_op jit(solution)/shard_map/all_gather | solution.py:137
  106.7 2.9 %fusion.8 = bf16[1024,512]{0,1:T(8,128)(2,1)S(1)} fusion(bf16[896,512]{1,0:T(8,128)(2,1)S(1)} %copy-done.3, bf16[1024,896]{1,0:T(8,128)(2,1)} %all-gather.8.cloned.1.call-done, f32[1024]{0:T(1024)S(1)} %bitcast.13), kind=kOutput, calls=%fused_computation.10 | convolution fusion | flops 942800896 | bytes 3805184 | tf_op jit(solution)/shard_map/dot_general | solution.py:142
  109.6 1.5 pad_maximum_fusion
  111.2 30.6 %reduce-scatter.3.cloned.1.call-done = bf16[256,1024]{0,1:T(8,128)(2,1)} async-done(((bf16[1024,1024]{0,1:T(8,128)(2,1)}), bf16[256,1024]{0,1:T(8,128)(2,1)}) %reduce-scatter.3.cloned.1.call-update) | async-done | bytes 524304 | tf_op jit(solution)/shard_map/reduce_scatter | solution.py:143
  141.8 1.1 convert_element_type.61
  143.2 2.5 collective-permute-start
  145.7 23.4 %collective-permute-done = bf16[256,1024]{0,1:T(8,128)(2,1)S(1)} collective-permute-done((bf16[256,1024]{0,1:T(8,128)(2,1)S(1)}, bf16[256,1024]{0,1:T(8,128)(2,1)S(1)}, u32[]{:S(2)}, u32[]{:S(2)}) %collective-permute-start) | collective-permute-done | bytes 524320 | tf_op jit(solution)/shard_map/ppermute | solution.py:10
  169.1 0.8 broadcast_select_fusion
  169.8 0.9 pad_maximum_fusion.1
  170.9 29.0 %all-gather.10.cloned.1.call-done = bf16[1024,1536]{0,1:T(8,128)(2,1)} async-done(((bf16[256,1536]{0,1:T(8,128)(2,1)}), bf16[1024,1536]{0,1:T(8,128)(2,1)}) %all-gather.10.cloned.1.call-update) | async-done | bytes 3145744 | tf_op jit(solution)/shard_map/all_gather | solution.py:152
  199.9 3.8 %convolution_convert_fusion = bf16[1024,896]{1,0:T(8,128)(2,1)} fusion(bf16[896,512]{1,0:T(8,128)(2,1)S(1)} %copy-done, bf16[1024,1536]{0,1:T(8,128)(2,1)} %all-gather.10.cloned.1.call-done), kind=kOutput, calls=%fused_computation.9 | convolution fusion | flops 940441600 | bytes 3801088 | tf_op jit(solution)/shard_map/nf,df->nd/dot_general | solution.py:154
  203.7 40.6 %all-gather.1 = bf16[32,1,256]{2,1,0:T(2,128)(2,1)S(1)} all-gather(bf16[1,1,256]{2,1,0:T(2,128)(2,1)S(1)} %reshape.28), channel_id=2, replica_groups=mesh['expert'=8,'dp'=4] {'expert','dp'}, dimensions={0}, use_global_device_ids=true | all-gather | bytes 16896 | tf_op jit(solution)/shard_map/all_gather | solution.py:146
  245.0 3.1 %fusion.14 = bf16[896,512]{0,1:T(8,128)(2,1)S(1)} fusion(bf16[1024,896]{1,0:T(8,128)(2,1)} %all-gather.6.cloned.1.call-done, bf16[1024,1536]{0,1:T(8,128)(2,1)} %all-gather.10.cloned.1.call-done), kind=kOutput, calls=%fused_computation.14 | convolution fusion | flops 939982848 | bytes 3801088 | tf_op jit(solution)/shard_map/nd,nf->df/dot_general | solution.py:155
  248.1 1.3 copy.21
  249.4 4.1 %fusion.11 = bf16[896,512]{1,0:T(8,128)(2,1)} fusion(bf16[1024,896]{1,0:T(8,128)(2,1)} %all-gather.8.cloned.1.call-done, f32[1024]{0:T(1024)S(1)} %bitcast.12, bf16[1024,1536]{0,1:T(8,128)(2,1)} %all-gather.10.cloned.1.call-done), kind=kOutput, calls=%fused_computation.12 | convolution fusion | flops 942735360 | bytes 3805184 | tf_op jit(solution)/shard_map/nd,nf->df/dot_general | solution.py:156
  253.5 17.0 %reduce-scatter.5.cloned.1.call-done = bf16[128,896]{1,0:T(8,128)(2,1)} async-done(((bf16[1024,896]{1,0:T(8,128)(2,1)}), bf16[128,896]{1,0:T(8,128)(2,1)}) %reduce-scatter.5.cloned.1.call-update) | async-done | bytes 229392 | tf_op jit(solution)/shard_map/reduce_scatter | solution.py:157
  (27 shorter events, 2.6 us)
Async XLA Ops:
  7.2 52.0 %copy-start = (bf16[896,512]{1,0:T(8,128)(2,1)S(1)}, bf16[896,512]{1,0:T(8,128)(2,1)}, u32[]{:S(2)}) copy-start(bf16[896,512]{1,0:T(8,128)(2,1)} %param.12) | copy-start | bytes 2752516
  7.2 52.0 %all-gather.6.cloned.1.call-start = ((), (), s32[]{:S(2)}) async-start(), calls=%async_computation.2 | async-start | bytes 2064384 | tf_op jit(solution)/shard_map/all_gather | solution.py:136
  7.9 98.7 %all-gather.8.cloned.1.call-start = ((), (), s32[]{:S(2)}) async-start(), calls=%async_computation.3 | async-start | bytes 2064384 | tf_op jit(solution)/shard_map/all_gather | solution.py:137
  8.7 133.1 %reduce-scatter.3.cloned.1.call-start = ((), (), s32[]{:S(2)}) async-start(), calls=%async_computation.4 | async-start | bytes 2621440 | tf_op jit(solution)/shard_map/reduce_scatter | solution.py:143
  40.8 65.9 %copy-start.3 = (bf16[896,512]{1,0:T(8,128)(2,1)S(1)}, bf16[896,512]{1,0:T(8,128)(2,1)}, u32[]{:S(2)}) copy-start(bf16[896,512]{1,0:T(8,128)(2,1)} %param.13) | copy-start | bytes 2752516
  111.1 88.7 %all-gather.10.cloned.1.call-start = ((), (), s32[]{:S(2)}) async-start(), calls=%async_computation.5 | async-start | bytes 3932160 | tf_op jit(solution)/shard_map/all_gather | solution.py:152
  143.2 25.9 %collective-permute-start = (bf16[256,1024]{0,1:T(8,128)(2,1)S(1)}, bf16[256,1024]{0,1:T(8,128)(2,1)S(1)}, u32[]{:S(2)}, u32[]{:S(2)}) collective-permute-start(bf16[256,1024]{0,1:T(8,128)(2,1)S(1)} %pad_maximum_fusion.2), channel_id=1, source_target_pairs={{0,16},{4,20},{8,24},{12,28},{16,0},{20,4},{24,8},{28,12},{1,17},{... | collective-permute-start | bytes 1572872 | tf_op jit(solution)/shard_map/ppermute | solution.py:10
  170.8 73.6 %copy-start.2 = (s32[128,2]{0,1:T(2,128)S(1)}, s32[128,2]{0,1:T(2,128)}, u32[]{:S(2)}) copy-start(s32[128,2]{0,1:T(2,128)} %param.8) | copy-start | bytes 3076
  170.8 73.6 %copy-start.1 = (f32[128,2]{0,1:T(2,128)S(1)}, f32[128,2]{0,1:T(2,128)}, u32[]{:S(2)}) copy-start(f32[128,2]{0,1:T(2,128)} %param.9) | copy-start | bytes 3076
  170.8 99.7 %reduce-scatter.5.cloned.1.call-start = ((), (), s32[]{:S(2)}) async-start(), calls=%async_computation.6 | async-start | bytes 2064384 | tf_op jit(solution)/shard_map/reduce_scatter | solution.py:157
Sparse Core Ops, SparseCore 0:
  10.2 48.9 all-gather.5
  61.3 45.2 all-gather.7
  111.3 30.4 reduce-scatter.2
  170.9 28.9 all-gather.9
  204.2 66.3 reduce-scatter.4

commit v2 on v0

--- a/solution.py
+++ b/solution.py
@@ -1,6 +1,9 @@
+import functools
 import jax
 import jax.numpy as jnp
 from jax import lax
+from jax.experimental import pallas as pl
+from jax.experimental.pallas import tpu as pltpu
 from jax.sharding import PartitionSpec as P
 
 
@@ -46,7 +49,9 @@
     scaled = scaled.reshape(-1, quarter)
     flat_routes = routes.reshape(-1)
     onehot = (flat_routes[:, None] == expert_ids[None, :]).astype(jnp.int32)
-    slot_rank = jnp.sum(jnp.cumsum(onehot, 0) * onehot, 1) - 1
+    route_order = jnp.arange(tok_rows * top_count, dtype=jnp.int32)
+    same = flat_routes[:, None] == flat_routes[None, :]
+    slot_rank = jnp.sum((same & (route_order[None, :] < route_order[:, None])).astype(jnp.int32), 1)
     own_weights = (w_up, w_down)
     shifted = passed_along((w_up, w_down), "expert", devices_ex // 2)
     resident = pick_pair(swapped_here, shifted, own_weights)
@@ -104,13 +109,366 @@
         ),
     )
     back_grid = back_rows.reshape(experts, 2, capacity, quarter)
-    picked = back_grid[target, :, slot_rank]
+    picked = [
+        back_grid[:, half].reshape(-1, quarter)[position].astype(jnp.float32) for half in range(2)
+    ]
     grad_tokens = jnp.sum(
-        picked.astype(jnp.float32).reshape(tok_rows, top_count * 2, quarter), 1
+        (picked[0] + picked[1]).reshape(tok_rows, top_count, quarter), 1
     ).astype(jnp.bfloat16)
     pair_grid = back_pairing.reshape(experts, 2, capacity)
     pair_picked = pair_grid[target, :, slot_rank]
     pairing_mine = jnp.sum(pair_picked.astype(jnp.float32), 1).reshape(tok_rows, top_count)
+    grad_logits = (1.0 - affinity) * (
+        pairing_mine - weights * jnp.sum(pairing_mine, -1, keepdims=True)
+    )
+    return (grad_tokens, grad_logits, grad_up, grad_down)
+
+def everything(
+    zs, dps, tok_ref, cot_ref, spread_ref, home_ref, slot_ref, swap_ref, up_ref, down_ref,
+    gt_ref, pair_ref, gu_ref, gd_ref,
+    rows_all, scaled_slot, part, part_in, mine, theirs, home_g, slot_g, back, back_x, back_z, to_z,
+    row_s, row_r, rs_s, rs_r, gh_s, gh_r, home_s, home_r, slot_s, slot_r, bx_s, bx_r, bz_s, bz_r,
+):
+    me = lax.axis_index("expert")
+    d = lax.axis_index("dp")
+    z, x = me // 2, me % 2
+    other = z * 2 + 1 - x
+    partner = ((z + zs // 2) % zs) * 2 + x
+    quarter = tok_ref.shape[1]
+    ff = up_ref.shape[1]
+    bf, f32 = jnp.bfloat16, jnp.float32
+
+    def remote(src, dst, send, recv, expert, dp):
+        return pltpu.make_async_remote_copy(
+            src_ref=src, dst_ref=dst, send_sem=send, recv_sem=recv,
+            device_id={"expert": expert, "dp": dp}, device_id_type=pl.DeviceIdType.MESH,
+        )
+
+    def peer(r):
+        return lax.rem(d + r, dps)
+
+    barrier = pltpu.get_barrier_semaphore()
+    for r in range(1, zs):
+        pl.semaphore_signal(
+            barrier, inc=1, device_id={"expert": ((z + r) % zs) * 2 + x, "dp": d},
+            device_id_type=pl.DeviceIdType.MESH,
+        )
+    pl.semaphore_signal(
+        barrier, inc=1, device_id={"expert": other, "dp": d}, device_id_type=pl.DeviceIdType.MESH
+    )
+    for r in range(1, dps):
+        pl.semaphore_signal(
+            barrier, inc=1, device_id={"expert": me, "dp": peer(r)},
+            device_id_type=pl.DeviceIdType.MESH,
+        )
+    rows_all[me, :, 0:quarter] = tok_ref[...]
+    rows_all[me, :, quarter : 2 * quarter] = cot_ref[...]
+    lanes = lax.broadcasted_iota(jnp.int32, spread_ref.shape, 1)
+    whole = spread_ref[...]
+    high = whole.astype(bf).astype(f32)
+    middle = (whole - high).astype(bf).astype(f32)
+    low = whole - high - middle
+    terms = jnp.where(lanes < 32, high, jnp.where(lanes < 64, middle, low))
+    rows_all[me, :, 2 * quarter :] = terms.astype(bf)
+    pl.semaphore_wait(barrier, zs - 1 + 1 + dps - 1)
+
+    def row_copy(b, way, expert):
+        return remote(
+            rows_all.at[b], rows_all.at[b], row_s.at[b, way], row_r.at[b], expert, d
+        )
+
+    def rs_copy(b, r):
+        return remote(
+            part.at[b, peer(r)], part_in.at[b, d], rs_s.at[b, r - 1], rs_r.at[b, d], me, peer(r)
+        )
+
+    def gh_copy(b):
+        return remote(mine.at[b], theirs.at[b], gh_s.at[b], gh_r.at[b], partner, d)
+
+    def home_copy(b, r):
+        return remote(
+            home_g.at[b, d], home_g.at[b, d], home_s.at[b, r - 1], home_r.at[b, d], me, peer(r)
+        )
+
+    def slot_copy(b, r):
+        return remote(
+            slot_g.at[b, d], slot_g.at[b, d], slot_s.at[b, r - 1], slot_r.at[b, d], me, peer(r)
+        )
+
+    def zz_of(j):
+        far = (j + 1) // 2
+        return jnp.where(j % 2 == 1, z + far, z - far)
+
+    def valid(j):
+        zz = zz_of(j)
+        return (j >= 0) & (j < 2 * zs - 1) & (zz >= 0) & (zz < zs)
+
+    def multiply(b):
+        ext = rows_all[b, :, 2 * quarter :].astype(f32)
+        cot = rows_all[b, :, quarter : 2 * quarter].astype(f32)
+        w_home = jnp.sum(ext * home_ref[...], axis=1, keepdims=True)
+        w_slot = jnp.sum(ext * slot_ref[...], axis=1, keepdims=True)
+        up = jnp.dot(rows_all[b, :, 0:quarter], up_ref[...], preferred_element_type=f32)
+        part[b, :, :, 0:ff] = up.astype(bf).reshape(dps, -1, ff)
+        scaled = (w_home * cot).astype(bf)
+        grad = jnp.dot(scaled, down_ref[...], preferred_element_type=f32)
+        part[b, :, :, ff:] = grad.astype(bf).reshape(dps, -1, ff)
+        for r in range(1, dps):
+            rs_copy(b, r).start()
+        scaled_slot[b] = (w_slot * cot).astype(bf)
+
+    def act(b):
+        for r in range(1, dps):
+            remote(
+                part.at[b, peer(r)], part_in.at[b, peer(r)], rs_s.at[b, r - 1],
+                rs_r.at[b, peer(r)], me, peer(r),
+            ).wait_recv()
+        total = part[b, d].astype(f32)
+        for r in range(1, dps):
+            total = total + part_in[b, peer(r)].astype(f32)
+        hidden, pairing, grad_pre = activate(total[:, 0:ff], total[:, ff:])
+        mine[b, :, 0:ff] = grad_pre
+        mine[b, :, ff:] = hidden
+        gh_copy(b).start()
+        at = lax.broadcasted_iota(jnp.int32, (grad_pre.shape[0], 128), 1)
+        home_g[b, d, :, 0:ff] = grad_pre
+        home_g[b, d, :, ff:] = jnp.where(at == z, pairing[:, None], 0.0).astype(bf)
+        for r in range(1, dps):
+            home_copy(b, r).start()
+
+    def first(j, _):
+        zz = zz_of(j)
+
+        @pl.when(valid(j))
+        def _():
+            b = zz * 2 + x
+
+            @pl.when(j > 0)
+            def _():
+                row_copy(b, 0, me).wait_recv()
+
+            @pl.when((zz <= z) & (z < zs - 1))
+            def _():
+                row_copy(b, 0, me + 2).start()
+
+            @pl.when((zz >= z) & (z > 0))
+            def _():
+                row_copy(b, 1, me - 2).start()
+
+            row_copy(b, 2, other).start()
+            multiply(b)
+
+        @pl.when(valid(j - 1))
+        def _():
+            b = zz_of(j - 1) * 2 + 1 - x
+            row_copy(b, 2, other).wait_recv()
+            multiply(b)
+            act(zz_of(j - 1) * 2 + x)
+
+        @pl.when(valid(j - 2))
+        def _():
+            act(zz_of(j - 2) * 2 + 1 - x)
+
+        return 0
+
+    lax.fori_loop(0, 2 * zs + 1, first, 0)
+
+    def second(j, _):
+        @pl.when(valid(j))
+        def _():
+            for side in range(2):
+                b = ((zz_of(j) + zs // 2) % zs) * 2 + side
+                gh_copy(b).wait_recv()
+                swap = swap_ref[...]
+                picked = mine[b].astype(f32) * (1.0 - swap) + theirs[b].astype(f32) * swap
+                slot_g[b, d] = picked.astype(bf)
+                for r in range(1, dps):
+                    slot_copy(b, r).start()
+
+        return 0
+
+    lax.fori_loop(0, 2 * zs - 1, second, 0)
+
+    def back_rows(b):
+        for r in range(1, dps):
+            remote(
+                home_g.at[b, d], home_g.at[b, peer(r)], home_s.at[b, r - 1],
+                home_r.at[b, peer(r)], me, peer(r),
+            ).wait_recv()
+        joined = home_g[b].reshape(-1, ff + 128)
+        rows = lax.dot_general(
+            joined[:, 0:ff], up_ref[...], (((1,), (1,)), ((), ())), preferred_element_type=f32
+        )
+        back[b, :, 0:quarter] = rows.astype(bf)
+        back[b, :, quarter:] = joined[:, ff:]
+
+    def bx_copy(zz):
+        return remote(
+            back.at[zz * 2 + 1 - x], back_x.at[zz], bx_s.at[zz], bx_r.at[zz], other, d
+        )
+
+    def bz_copy(zz):
+        return remote(to_z.at[zz], back_z.at[z], bz_s.at[zz], bz_r.at[z], zz * 2 + x, d)
+
+    def third(r, _):
+        zz = (z + r) % zs
+        back_rows(zz * 2 + 1 - x)
+        bx_copy(zz).start()
+        return 0
+
+    lax.fori_loop(1, zs + 1, third, 0)
+
+    def fourth(r, _):
+        zz = (z + r) % zs
+        b = zz * 2 + x
+        back_rows(b)
+        bx_copy(zz).wait_recv()
+        both = (back[b].astype(f32) + back_x[zz].astype(f32)).astype(bf)
+
+        @pl.when(zz != z)
+        def _():
+            to_z[zz] = both
+            bz_copy(zz).start()
+
+        @pl.when(zz == z)
+        def _():
+            back_z[z] = both
+
+        return 0
+
+    lax.fori_loop(1, zs + 1, fourth, 0)
+
+    def slot_wait(b, _):
+        for r in range(1, dps):
+            remote(
+                slot_g.at[b, d], slot_g.at[b, peer(r)], slot_s.at[b, r - 1],
+                slot_r.at[b, peer(r)], me, peer(r),
+            ).wait_recv()
+        return 0
+
+    lax.fori_loop(0, 2 * zs, slot_wait, 0)
+
+    def weight_grads(c, _):
+        at = pl.ds(pl.multiple_of(c * 128, 128), 128)
+        tokens = rows_all[:, :, at].reshape(-1, 128)
+        gu_ref[at, :] = lax.dot_general(
+            tokens, slot_g[:, :, :, 0:ff].reshape(-1, ff), (((0,), (0,)), ((), ())),
+            preferred_element_type=f32,
+        ).astype(bf)
+        scaled = scaled_slot[:, :, at].reshape(-1, 128)
+        gd_ref[at, :] = lax.dot_general(
+            scaled, slot_g[:, :, :, ff:].reshape(-1, ff), (((0,), (0,)), ((), ())),
+            preferred_element_type=f32,
+        ).astype(bf)
+        return 0
+
+    lax.fori_loop(0, quarter // 128, weight_grads, 0)
+
+    for r in range(1, zs):
+        zz = (z + r) % zs
+        remote(to_z.at[zz], back_z.at[zz], bz_s.at[zz], bz_r.at[zz], zz * 2 + x, d).wait_recv()
+    total = back_z[0].astype(f32)
+    for r in range(1, zs):
+        total = total + back_z[r].astype(f32)
+    gt_ref[...] = total[:, 0:quarter].astype(bf)
+    pair_ref[...] = total[:, quarter:]
+
+    def drain(b, _):
+        zz = b // 2
+
+        @pl.when(b % 2 == x)
+        def _():
+            @pl.when((zz <= z) & (z < zs - 1))
+            def _():
+                row_copy(b, 0, me + 2).wait_send()
+
+            @pl.when((zz >= z) & (z > 0))
+            def _():
+                row_copy(b, 1, me - 2).wait_send()
+
+            row_copy(b, 2, other).wait_send()
+
+            @pl.when(zz != z)
+            def _():
+                bz_copy(zz).wait_send()
+
+            bx_copy(zz).wait_send()
+
+        for r in range(1, dps):
+            rs_copy(b, r).wait_send()
+            home_copy(b, r).wait_send()
+            slot_copy(b, r).wait_send()
+        gh_copy(b).wait_send()
+        return 0
+
+    lax.fori_loop(0, 2 * zs, drain, 0)
+
+
+def one_kernel(tokens, routes, logits, cotangent, pair_flags, w_up, w_down):
+    devices_ex = lax.axis_size("expert")
+    dps = lax.axis_size("dp")
+    experts = devices_ex // 2
+    half_way = experts // 2
+    slot_here = lax.axis_index("expert") // 2
+    tok_rows, top_count = routes.shape
+    quarter = tokens.shape[1]
+    ff = w_up.shape[1]
+    expert_ids = jnp.arange(experts, dtype=jnp.int32)
+    paired = jnp.concatenate([pair_flags, pair_flags]) > 0
+    swapped_here = paired[slot_here]
+    owner_here = jnp.where(swapped_here, (slot_here + half_way) % experts, slot_here)
+    affinity = jax.nn.sigmoid(logits)
+    weights = affinity / jnp.sum(affinity, -1, keepdims=True)
+    lanes = jnp.arange(128, dtype=jnp.int32)
+    group = jnp.where(lanes < 96, lanes % 32, 32)
+    spread = jnp.zeros((tok_rows, 128), jnp.float32)
+    for k in range(top_count):
+        spread = spread + jnp.where(routes[:, k : k + 1] == group[None, :], weights[:, k : k + 1], 0.0)
+    pick_home = (group == slot_here).astype(jnp.float32)[None, :]
+    pick_slot = (group == owner_here).astype(jnp.float32)[None, :]
+    swap = jnp.broadcast_to(swapped_here.astype(jnp.float32), (1, 2 * ff))
+    bf = jnp.bfloat16
+    part_rows = tok_rows // dps
+    vmem = pl.BlockSpec(memory_space=pltpu.VMEM)
+    dma = pltpu.SemaphoreType.DMA
+    n = devices_ex
+    grad_tokens, pairs, grad_up, grad_down = pl.pallas_call(
+        functools.partial(everything, experts, dps),
+        out_shape=(
+            jax.ShapeDtypeStruct((tok_rows, quarter), bf),
+            jax.ShapeDtypeStruct((tok_rows, 128), jnp.float32),
+            jax.ShapeDtypeStruct((quarter, ff), bf),
+            jax.ShapeDtypeStruct((quarter, ff), bf),
+        ),
+        in_specs=[vmem] * 8,
+        out_specs=(vmem,) * 4,
+        scratch_shapes=[
+            pltpu.VMEM((n, tok_rows, 2 * quarter + 128), bf),
+            pltpu.VMEM((n, tok_rows, quarter), bf),
+            pltpu.VMEM((n, dps, part_rows, 2 * ff), bf),
+            pltpu.VMEM((n, dps, part_rows, 2 * ff), bf),
+            pltpu.VMEM((n, part_rows, 2 * ff), bf),
+            pltpu.VMEM((n, part_rows, 2 * ff), bf),
+            pltpu.VMEM((n, dps, part_rows, ff + 128), bf),
+            pltpu.VMEM((n, dps, part_rows, 2 * ff), bf),
+            pltpu.VMEM((n, tok_rows, quarter + 128), bf),
+            pltpu.VMEM((experts, tok_rows, quarter + 128), bf),
+            pltpu.VMEM((experts, tok_rows, quarter + 128), bf),
+            pltpu.VMEM((experts, tok_rows, quarter + 128), bf),
+            dma((n, 3)), dma((n,)),
+            dma((n, dps - 1)), dma((n, dps)),
+            dma((n,)), dma((n,)),
+            dma((n, dps - 1)), dma((n, dps)),
+            dma((n, dps - 1)), dma((n, dps)),
+            dma((experts,)), dma((experts,)),
+            dma((experts,)), dma((experts,)),
+        ],
+        compiler_params=pltpu.CompilerParams(
+            collective_id=0, has_side_effects=True, vmem_limit_bytes=56 * 1024 * 1024
+        ),
+    )(tokens, cotangent, spread, pick_home, pick_slot, swap, w_up, w_down)
+    chosen = (routes[:, :, None] == expert_ids[None, None, :]).astype(jnp.float32)
+    pairing_mine = jnp.sum(chosen * pairs[:, None, 0:experts], -1)
     grad_logits = (1.0 - affinity) * (
         pairing_mine - weights * jnp.sum(pairing_mine, -1, keepdims=True)
     )
@@ -127,5 +485,6 @@
         P("dp", "expert"),
         P("dp", "expert"),
     )
+    body = one_kernel if mesh.shape["expert"] <= 8 else local
     out_specs = (P("expert", "dp"), P("expert", None), P("dp", "expert"), P("dp", "expert"))
-    return jax.shard_map(local, mesh=mesh, in_specs=in_specs, out_specs=out_specs, check_vma=False)
+    return jax.shard_map(body, mesh=mesh, in_specs=in_specs, out_specs=out_specs, check_vma=False)

time: 292 us -> 126 us (0.43)
  the two profiles are of different devices: /device:TPU:0 before, /device:TPU:11 now
where the time goes in v2:
time: 126 us
  Pallas kernels  113 us (90%)
  local copies, waits for them, and re-layouts  8.88 us (7%)
  other arithmetic  2.02 us (2%)
  between operations  2.01 us (2%)
    pallas_call x1, Pallas kernels, one_kernel(): pl.pallas_call(functools.partial(everything, experts, dps), out_shape=(ja...  113 us
    unnamed x11, local copies, waits for them, and re-layouts  6.78 us

profile of v2, /device:TPU:11, one launch (start us, length us, event | category | flops | bytes accessed | tf_op | source)
XLA Modules:
  0.0 126.1 jit_solution(8431412009201115326)
XLA Ops:
  0.7 0.0 copy-start.2
  0.7 0.7 copy-done.2
  1.3 0.0 copy-start.3
  1.4 0.6 copy-done.3
  2.0 0.1 add_compare_fusion
  2.1 0.6 dynamic_slice.3
  4.0 0.5 compare_convert_fusion
  4.5 0.0 copy-start.1
  4.5 0.7 copy-done.1
  5.2 0.6 broadcast_in_dim.41.swap_ref
  5.8 0.8 select_add_fusion.spread_ref
  6.6 113.2 %shard_map.102 = (bf16[128,896]{1,0:T(8,128)(2,1)}, f32[128,128]{1,0:T(8,128)}, bf16[896,512]{1,0:T(8,128)(2,1)}, bf16[896,512]{1,0:T(8,128)(2,1)}) custom-call(bf16[128,896]{1,0:T(8,128)(2,1)} %tok_ref.1, bf16[128,896]{1,0:T(8,128)(2,1)} %cot_ref.1, f32[128,128]{1,0:T(8,128)} %select_add_fusion.spread_ref, f32[1,128]{1,0:T(1,128)} %get-tuple-element.19.home_ref, ...), custom_call_target="tpu_custom_call" | custom-call | tf_op jit(solution)/shard_map/pallas_call | solution.py:435
  119.7 0.9 copy.12
  120.7 0.6 subtract_multiply_fusion
  121.3 1.6 %copy.16 = bf16[128,896]{1,0:T(8,128)(2,1)} copy(bf16[128,896]{1,0:T(8,128)(2,1)} %get-tuple-element.24) | data formatting | bytes 458752
  122.9 0.0 copy-start
  122.9 2.2 %copy.17 = bf16[896,512]{1,0:T(8,128)(2,1)} copy(bf16[896,512]{1,0:T(8,128)(2,1)} %get-tuple-element.26) | data formatting | bytes 1835008
  125.2 0.0 copy-done
  125.2 0.9 copy.18
  (6 shorter events, 0.1 us)
Async XLA Ops:
  0.7 0.7 copy-start.2
  1.3 0.7 copy-start.3
  4.5 0.7 copy-start.1
  122.9 2.2 %copy-start = (bf16[896,512]{1,0:T(8,128)(2,1)S(1)}, bf16[896,512]{1,0:T(8,128)(2,1)}, u32[]{:S(2)}) copy-start(bf16[896,512]{1,0:T(8,128)(2,1)} %get-tuple-element.27) | copy-start | bytes 2752516

commit v3 on v2

--- a/solution.py
+++ b/solution.py
@@ -124,10 +124,11 @@
     return (grad_tokens, grad_logits, grad_up, grad_down)
 
 def everything(
-    zs, dps, tok_ref, cot_ref, spread_ref, home_ref, slot_ref, swap_ref, up_ref, down_ref,
-    gt_ref, pair_ref, gu_ref, gd_ref,
+    zs, dps, tok_ref, cot_ref, routes_ref, logits_ref, flags_ref, up_hbm, down_hbm,
+    gt_ref, gl_ref, gu_ref, gd_ref,
+    up_ref, down_ref,
     rows_all, scaled_slot, part, part_in, mine, theirs, home_g, slot_g, back, back_x, back_z, to_z,
-    row_s, row_r, rs_s, rs_r, gh_s, gh_r, home_s, home_r, slot_s, slot_r, bx_s, bx_r, bz_s, bz_r,
+    row_s, row_r, rs_s, rs_r, gh_s, gh_r, home_s, home_r, slot_s, slot_r, bx_s, bx_r, bz_s, bz_r, local_s,
 ):
     me = lax.axis_index("expert")
     d = lax.axis_index("dp")
@@ -161,15 +162,37 @@
             barrier, inc=1, device_id={"expert": me, "dp": peer(r)},
             device_id_type=pl.DeviceIdType.MESH,
         )
-    rows_all[me, :, 0:quarter] = tok_ref[...]
-    rows_all[me, :, quarter : 2 * quarter] = cot_ref[...]
-    lanes = lax.broadcasted_iota(jnp.int32, spread_ref.shape, 1)
-    whole = spread_ref[...]
+    held = [
+        pltpu.make_async_copy(tok_ref, rows_all.at[me, :, 0:quarter], local_s.at[0]),
+        pltpu.make_async_copy(cot_ref, rows_all.at[me, :, quarter : 2 * quarter], local_s.at[1]),
+        pltpu.make_async_copy(up_hbm, up_ref, local_s.at[2]),
+        pltpu.make_async_copy(down_hbm, down_ref, local_s.at[3]),
+    ]
+    for copy in held:
+        copy.start()
+    affinity = jax.nn.sigmoid(logits_ref[...])
+    weights = affinity / jnp.sum(affinity, -1, keepdims=True)
+    lanes = lax.broadcasted_iota(jnp.int32, (tok_ref.shape[0], 128), 1)
+    group = jnp.where(lanes < 96, lanes % 32, 32)
+    tops = logits_ref.shape[1]
+    whole = jnp.zeros(lanes.shape, f32)
+    for k in range(tops):
+        whole = whole + jnp.where(routes_ref[:, k : k + 1] == group, weights[:, k : k + 1], 0.0)
+    pair_lane = lax.broadcasted_iota(jnp.int32, flags_ref.shape, 1)
+    swap = jnp.sum(
+        jnp.where((pair_lane == z % (zs // 2)) & (flags_ref[...] > 0), 1.0, 0.0), 1, keepdims=True
+    )
+    group_row = group[0:1, :]
+    pick_home = jnp.where(group_row == z, 1.0, 0.0)
+    pick_far = jnp.where(group_row == (z + zs // 2) % zs, 1.0, 0.0)
+    pick_slot = pick_home * (1.0 - swap) + pick_far * swap
     high = whole.astype(bf).astype(f32)
     middle = (whole - high).astype(bf).astype(f32)
     low = whole - high - middle
     terms = jnp.where(lanes < 32, high, jnp.where(lanes < 64, middle, low))
     rows_all[me, :, 2 * quarter :] = terms.astype(bf)
+    for copy in held:
+        copy.wait()
     pl.semaphore_wait(barrier, zs - 1 + 1 + dps - 1)
 
     def row_copy(b, way, expert):
@@ -190,10 +213,22 @@
             home_g.at[b, d], home_g.at[b, d], home_s.at[b, r - 1], home_r.at[b, d], me, peer(r)
         )
 
-    def slot_copy(b, r):
+    core = d + 1 - 2 * (d % 2)
+    across = (d + 2) % 4
+    corner = (core + 2) % 4
+
+    def slot_copy(b, way):
+        piece = across if way == 2 else d
+        target = across if way == 1 else core
         return remote(
-            slot_g.at[b, d], slot_g.at[b, d], slot_s.at[b, r - 1], slot_r.at[b, d], me, peer(r)
-        )
+            slot_g.at[b, piece], slot_g.at[b, piece], slot_s.at[b, way], slot_r.at[b, piece],
+            me, target,
+        )
+
+    def slot_wait(b, piece, source):
+        remote(
+            slot_g.at[b, d], slot_g.at[b, piece], slot_s.at[b, 0], slot_r.at[b, piece], me, source
+        ).wait_recv()
 
     def zz_of(j):
         far = (j + 1) // 2
@@ -206,8 +241,8 @@
     def multiply(b):
         ext = rows_all[b, :, 2 * quarter :].astype(f32)
         cot = rows_all[b, :, quarter : 2 * quarter].astype(f32)
-        w_home = jnp.sum(ext * home_ref[...], axis=1, keepdims=True)
-        w_slot = jnp.sum(ext * slot_ref[...], axis=1, keepdims=True)
+        w_home = jnp.sum(ext * pick_home, axis=1, keepdims=True)
+        w_slot = jnp.sum(ext * pick_slot, axis=1, keepdims=True)
         up = jnp.dot(rows_all[b, :, 0:quarter], up_ref[...], preferred_element_type=f32)
         part[b, :, :, 0:ff] = up.astype(bf).reshape(dps, -1, ff)
         scaled = (w_home * cot).astype(bf)
@@ -236,59 +271,6 @@
         for r in range(1, dps):
             home_copy(b, r).start()
 
-    def first(j, _):
-        zz = zz_of(j)
-
-        @pl.when(valid(j))
-        def _():
-            b = zz * 2 + x
-
-            @pl.when(j > 0)
-            def _():
-                row_copy(b, 0, me).wait_recv()
-
-            @pl.when((zz <= z) & (z < zs - 1))
-            def _():
-                row_copy(b, 0, me + 2).start()
-
-            @pl.when((zz >= z) & (z > 0))
-            def _():
-                row_copy(b, 1, me - 2).start()
-
-            row_copy(b, 2, other).start()
-            multiply(b)
-
-        @pl.when(valid(j - 1))
-        def _():
-            b = zz_of(j - 1) * 2 + 1 - x
-            row_copy(b, 2, other).wait_recv()
-            multiply(b)
-            act(zz_of(j - 1) * 2 + x)
-
-        @pl.when(valid(j - 2))
-        def _():
-            act(zz_of(j - 2) * 2 + 1 - x)
-
-        return 0
-
-    lax.fori_loop(0, 2 * zs + 1, first, 0)
-
-    def second(j, _):
-        @pl.when(valid(j))
-        def _():
-            for side in range(2):
-                b = ((zz_of(j) + zs // 2) % zs) * 2 + side
-                gh_copy(b).wait_recv()
-                swap = swap_ref[...]
-                picked = mine[b].astype(f32) * (1.0 - swap) + theirs[b].astype(f32) * swap
-                slot_g[b, d] = picked.astype(bf)
-                for r in range(1, dps):
-                    slot_copy(b, r).start()
-
-        return 0
-
-    lax.fori_loop(0, 2 * zs - 1, second, 0)
-
     def back_rows(b):
         for r in range(1, dps):
             remote(
@@ -310,43 +292,100 @@
     def bz_copy(zz):
         return remote(to_z.at[zz], back_z.at[z], bz_s.at[zz], bz_r.at[z], zz * 2 + x, d)
 
-    def third(r, _):
-        zz = (z + r) % zs
-        back_rows(zz * 2 + 1 - x)
-        bx_copy(zz).start()
+    def first(j, _):
+        zz = zz_of(j)
+
+        @pl.when(valid(j))
+        def _():
+            b = zz * 2 + x
+
+            @pl.when(j > 0)
+            def _():
+                row_copy(b, 0, me).wait_recv()
+
+            @pl.when((zz <= z) & (z < zs - 1))
+            def _():
+                row_copy(b, 0, me + 2).start()
+
+            @pl.when((zz >= z) & (z > 0))
+            def _():
+                row_copy(b, 1, me - 2).start()
+
+            row_copy(b, 2, other).start()
+            multiply(b)
+
+        @pl.when(valid(j - 1))
+        def _():
+            b = zz_of(j - 1) * 2 + 1 - x
+            row_copy(b, 2, other).wait_recv()
+            multiply(b)
+            act(zz_of(j - 1) * 2 + x)
+
+        @pl.when(valid(j - 2))
+        def _():
+            act(zz_of(j - 2) * 2 + 1 - x)
+            back_rows(zz_of(j - 2) * 2 + x)
+
+        @pl.when(valid(j - 3))
+        def _():
+            back_rows(zz_of(j - 3) * 2 + 1 - x)
+            bx_copy(zz_of(j - 3)).start()
+
         return 0
 
-    lax.fori_loop(1, zs + 1, third, 0)
-
-    def fourth(r, _):
-        zz = (z + r) % zs
+    lax.fori_loop(0, 2 * zs + 2, first, 0)
+
+    def slot_forward(b):
+        slot_wait(b, across, across)
+        slot_copy(b, 2).start()
+
+    def second(j, _):
+        @pl.when(valid(j))
+        def _():
+            for side in range(2):
+                b = ((zz_of(j) + zs // 2) % zs) * 2 + side
+                gh_copy(b).wait_recv()
+                picked = mine[b].astype(f32) * (1.0 - swap) + theirs[b].astype(f32) * swap
+                slot_g[b, d] = picked.astype(bf)
+                slot_copy(b, 1).start()
+                slot_copy(b, 0).start()
+
+        @pl.when(valid(j - 1))
+        def _():
+            for side in range(2):
+                slot_forward(((zz_of(j - 1) + zs // 2) % zs) * 2 + side)
+
+        return 0
+
+    lax.fori_loop(0, 2 * zs, second, 0)
+
+    def fourth(j, _):
+        zz = zz_of(j)
         b = zz * 2 + x
-        back_rows(b)
-        bx_copy(zz).wait_recv()
-        both = (back[b].astype(f32) + back_x[zz].astype(f32)).astype(bf)
-
-        @pl.when(zz != z)
-        def _():
-            to_z[zz] = both
+
+        @pl.when(valid(j))
+        def _():
+            bx_copy(zz).wait_recv()
+
+        @pl.when(valid(j) & (zz != z))
+        def _():
+            to_z[zz] = (back[b].astype(f32) + back_x[zz].astype(f32)).astype(bf)
             bz_copy(zz).start()
 
-        @pl.when(zz == z)
-        def _():
-            back_z[z] = both
+        @pl.when(valid(j) & (zz == z))
+        def _():
+            back_z[z] = (back[b].astype(f32) + back_x[zz].astype(f32)).astype(bf)
 
         return 0
 
-    lax.fori_loop(1, zs + 1, fourth, 0)
-
-    def slot_wait(b, _):
-        for r in range(1, dps):
-            remote(
-                slot_g.at[b, d], slot_g.at[b, peer(r)], slot_s.at[b, r - 1],
-                slot_r.at[b, peer(r)], me, peer(r),
-            ).wait_recv()
+    lax.fori_loop(0, 2 * zs - 1, fourth, 0)
+
+    def slot_rest(b, _):
+        slot_wait(b, core, core)
+        slot_wait(b, corner, core)
         return 0
 
-    lax.fori_loop(0, 2 * zs, slot_wait, 0)
+    lax.fori_loop(0, 2 * zs, slot_rest, 0)
 
     def weight_grads(c, _):
         at = pl.ds(pl.multiple_of(c * 128, 128), 128)
@@ -371,7 +410,16 @@
     for r in range(1, zs):
         total = total + back_z[r].astype(f32)
     gt_ref[...] = total[:, 0:quarter].astype(bf)
-    pair_ref[...] = total[:, quarter:]
+    pairs = total[:, quarter:]
+    pairing = [
+        jnp.sum(jnp.where(lanes == routes_ref[:, k : k + 1], pairs, 0.0), 1, keepdims=True)
+        for k in range(tops)
+    ]
+    across_k = sum(pairing[1:], pairing[0])
+    for k in range(tops):
+        gl_ref[:, k : k + 1] = (1.0 - affinity[:, k : k + 1]) * (
+            pairing[k] - weights[:, k : k + 1] * across_k
+        )
 
     def drain(b, _):
         zz = b // 2
@@ -397,7 +445,7 @@
         for r in range(1, dps):
             rs_copy(b, r).wait_send()
             home_copy(b, r).wait_send()
-            slot_copy(b, r).wait_send()
+            slot_copy(b, r - 1).wait_send()
         gh_copy(b).wait_send()
         return 0
 
@@ -408,41 +456,28 @@
     devices_ex = lax.axis_size("expert")
     dps = lax.axis_size("dp")
     experts = devices_ex // 2
-    half_way = experts // 2
-    slot_here = lax.axis_index("expert") // 2
-    tok_rows, top_count = routes.shape
+    tok_rows = routes.shape[0]
     quarter = tokens.shape[1]
     ff = w_up.shape[1]
-    expert_ids = jnp.arange(experts, dtype=jnp.int32)
-    paired = jnp.concatenate([pair_flags, pair_flags]) > 0
-    swapped_here = paired[slot_here]
-    owner_here = jnp.where(swapped_here, (slot_here + half_way) % experts, slot_here)
-    affinity = jax.nn.sigmoid(logits)
-    weights = affinity / jnp.sum(affinity, -1, keepdims=True)
-    lanes = jnp.arange(128, dtype=jnp.int32)
-    group = jnp.where(lanes < 96, lanes % 32, 32)
-    spread = jnp.zeros((tok_rows, 128), jnp.float32)
-    for k in range(top_count):
-        spread = spread + jnp.where(routes[:, k : k + 1] == group[None, :], weights[:, k : k + 1], 0.0)
-    pick_home = (group == slot_here).astype(jnp.float32)[None, :]
-    pick_slot = (group == owner_here).astype(jnp.float32)[None, :]
-    swap = jnp.broadcast_to(swapped_here.astype(jnp.float32), (1, 2 * ff))
     bf = jnp.bfloat16
     part_rows = tok_rows // dps
     vmem = pl.BlockSpec(memory_space=pltpu.VMEM)
+    hbm = pl.BlockSpec(memory_space=pl.ANY)
     dma = pltpu.SemaphoreType.DMA
     n = devices_ex
-    grad_tokens, pairs, grad_up, grad_down = pl.pallas_call(
+    return pl.pallas_call(
         functools.partial(everything, experts, dps),
         out_shape=(
             jax.ShapeDtypeStruct((tok_rows, quarter), bf),
-            jax.ShapeDtypeStruct((tok_rows, 128), jnp.float32),
+            jax.ShapeDtypeStruct(logits.shape, jnp.float32),
             jax.ShapeDtypeStruct((quarter, ff), bf),
             jax.ShapeDtypeStruct((quarter, ff), bf),
         ),
-        in_specs=[vmem] * 8,
+        in_specs=[hbm, hbm, vmem, vmem, vmem, hbm, hbm],
         out_specs=(vmem,) * 4,
         scratch_shapes=[
+            pltpu.VMEM(w_up.shape, bf),
+            pltpu.VMEM(w_down.shape, bf),
             pltpu.VMEM((n, tok_rows, 2 * quarter + 128), bf),
             pltpu.VMEM((n, tok_rows, quarter), bf),
             pltpu.VMEM((n, dps, part_rows, 2 * ff), bf),
@@ -461,18 +496,12 @@
             dma((n, dps - 1)), dma((n, dps)),
             dma((n, dps - 1)), dma((n, dps)),
             dma((experts,)), dma((experts,)),
-            dma((experts,)), dma((experts,)),
+            dma((experts,)), dma((experts,)), dma((4,)),
         ],
         compiler_params=pltpu.CompilerParams(
             collective_id=0, has_side_effects=True, vmem_limit_bytes=56 * 1024 * 1024
         ),
-    )(tokens, cotangent, spread, pick_home, pick_slot, swap, w_up, w_down)
-    chosen = (routes[:, :, None] == expert_ids[None, None, :]).astype(jnp.float32)
-    pairing_mine = jnp.sum(chosen * pairs[:, None, 0:experts], -1)
-    grad_logits = (1.0 - affinity) * (
-        pairing_mine - weights * jnp.sum(pairing_mine, -1, keepdims=True)
-    )
-    return (grad_tokens, grad_logits, grad_up, grad_down)
+    )(tokens, cotangent, routes, logits, pair_flags.reshape(1, -1), w_up, w_down)
 
 
 def solution(mesh):
@@ -485,6 +514,7 @@
         P("dp", "expert"),
         P("dp", "expert"),
     )
-    body = one_kernel if mesh.shape["expert"] <= 8 else local
+    small = mesh.shape["expert"] == 8 and mesh.shape["dp"] == 4
+    body = one_kernel if small else local
     out_specs = (P("expert", "dp"), P("expert", None), P("dp", "expert"), P("dp", "expert"))
     return jax.shard_map(body, mesh=mesh, in_specs=in_specs, out_specs=out_specs, check_vma=False)

time: 126 us -> 125 us (level)
  the two profiles are of different devices: /device:TPU:11 before, /device:TPU:0 now
where the time goes in v3:
time: 125 us; the launch traced here: 124 us
  Pallas kernels  115 us (92%)
  local copies, waits for them, and re-layouts  8.44 us (7%)
    pallas_call x1, Pallas kernels, one_kernel(): pl.pallas_call(functools.partial(everything, experts, dps), out_shape=(ja...  115 us
    unnamed x11, local copies, waits for them, and re-layouts  6.97 us

profile of v3, /device:TPU:0, one launch (start us, length us, event | category | flops | bytes accessed | tf_op | source)
XLA Modules:
  0.0 124.2 jit_solution(16508303172308428681)
XLA Ops:
  0.6 0.0 copy-start.1
  0.6 0.7 copy-done.1
  1.3 0.0 copy-start.2
  1.3 0.7 copy.11.routes_ref
  2.1 0.0 copy-done.2
  2.1 0.7 copy.12.logits_ref
  2.8 115.1 %shard_map.102 = (bf16[128,896]{1,0:T(8,128)(2,1)}, f32[128,2]{1,0:T(8,128)}, bf16[896,512]{1,0:T(8,128)(2,1)}, bf16[896,512]{1,0:T(8,128)(2,1)}) custom-call(bf16[128,896]{1,0:T(8,128)(2,1)} %tok_ref.1, bf16[128,896]{1,0:T(8,128)(2,1)} %cot_ref.1, s32[128,2]{1,0:T(8,128)} %copy.11.routes_ref, f32[128,2]{1,0:T(8,128)} %copy.12.logits_ref, s32[1,2]{1,0:T(1,128)} %bitcast.1, ...), custom_call_target="tpu_custom_call" | custom-call | tf_op jit(solution)/shard_map/pallas_call | solution.py:468
  117.9 1.5 %copy.13 = f32[128,2]{0,1:T(2,128)} copy(f32[128,2]{1,0:T(8,128)} %get-tuple-element.5) | data formatting | bytes 2048 | tf_op jit(solution)/shard_map/pallas_call | solution.py:468
  119.3 1.6 %copy.17 = bf16[128,896]{1,0:T(8,128)(2,1)} copy(bf16[128,896]{1,0:T(8,128)(2,1)} %get-tuple-element.12) | data formatting | bytes 458752
  121.0 0.0 copy-start
  121.0 2.2 %copy.18 = bf16[896,512]{1,0:T(8,128)(2,1)} copy(bf16[896,512]{1,0:T(8,128)(2,1)} %get-tuple-element.14) | data formatting | bytes 1835008
  123.2 0.0 copy-done
  123.2 0.9 copy.19
Async XLA Ops:
  0.6 0.7 copy-start.1
  1.3 0.7 copy-start.2
  121.0 2.2 %copy-start = (bf16[896,512]{1,0:T(8,128)(2,1)S(1)}, bf16[896,512]{1,0:T(8,128)(2,1)}, u32[]{:S(2)}) copy-start(bf16[896,512]{1,0:T(8,128)(2,1)} %get-tuple-element.15) | copy-start | bytes 2752516

commit v4 on v3

--- a/solution.py
+++ b/solution.py
@@ -387,21 +387,18 @@
 
     lax.fori_loop(0, 2 * zs, slot_rest, 0)
 
-    def weight_grads(c, _):
-        at = pl.ds(pl.multiple_of(c * 128, 128), 128)
-        tokens = rows_all[:, :, at].reshape(-1, 128)
+    for low_at in range(0, quarter, 512):
+        at = slice(low_at, min(low_at + 512, quarter))
+        tokens = rows_all[:, :, at].reshape(-1, at.stop - at.start)
         gu_ref[at, :] = lax.dot_general(
             tokens, slot_g[:, :, :, 0:ff].reshape(-1, ff), (((0,), (0,)), ((), ())),
             preferred_element_type=f32,
         ).astype(bf)
-        scaled = scaled_slot[:, :, at].reshape(-1, 128)
+        scaled = scaled_slot[:, :, at].reshape(-1, at.stop - at.start)
         gd_ref[at, :] = lax.dot_general(
             scaled, slot_g[:, :, :, ff:].reshape(-1, ff), (((0,), (0,)), ((), ())),
             preferred_element_type=f32,
         ).astype(bf)
-        return 0
-
-    lax.fori_loop(0, quarter // 128, weight_grads, 0)
 
     for r in range(1, zs):
         zz = (z + r) % zs

time: 125 us -> 125 us (level)
  no operation moved by 1% of the time
where the time goes in v4:
time: 125 us; the launch traced here: 124 us
  Pallas kernels  115 us (92%)
  local copies, waits for them, and re-layouts  8.44 us (7%)
    pallas_call x1, Pallas kernels, one_kernel(): pl.pallas_call(functools.partial(everything, experts, dps), out_shape=(ja...  115 us
    unnamed x11, local copies, waits for them, and re-layouts  6.97 us

profile of v4, /device:TPU:0, one launch (start us, length us, event | category | flops | bytes accessed | tf_op | source)
XLA Modules:
  0.0 124.2 jit_solution(5203581445137769137)
XLA Ops:
  0.6 0.0 copy-start.1
  0.6 0.7 copy-done.1
  1.3 0.0 copy-start.2
  1.3 0.7 copy.11.routes_ref
  2.1 0.0 copy-done.2
  2.1 0.7 copy.12.logits_ref
  2.8 115.1 %shard_map.102 = (bf16[128,896]{1,0:T(8,128)(2,1)}, f32[128,2]{1,0:T(8,128)}, bf16[896,512]{1,0:T(8,128)(2,1)}, bf16[896,512]{1,0:T(8,128)(2,1)}) custom-call(bf16[128,896]{1,0:T(8,128)(2,1)} %tok_ref.1, bf16[128,896]{1,0:T(8,128)(2,1)} %cot_ref.1, s32[128,2]{1,0:T(8,128)} %copy.11.routes_ref, f32[128,2]{1,0:T(8,128)} %copy.12.logits_ref, s32[1,2]{1,0:T(1,128)} %bitcast.1, ...), custom_call_target="tpu_custom_call" | custom-call | tf_op jit(solution)/shard_map/pallas_call | solution.py:465
  117.9 1.5 %copy.13 = f32[128,2]{0,1:T(2,128)} copy(f32[128,2]{1,0:T(8,128)} %get-tuple-element.5) | data formatting | bytes 2048 | tf_op jit(solution)/shard_map/pallas_call | solution.py:465
  119.3 1.6 %copy.17 = bf16[128,896]{1,0:T(8,128)(2,1)} copy(bf16[128,896]{1,0:T(8,128)(2,1)} %get-tuple-element.12) | data formatting | bytes 458752
  121.0 0.0 copy-start
  121.0 2.2 %copy.18 = bf16[896,512]{1,0:T(8,128)(2,1)} copy(bf16[896,512]{1,0:T(8,128)(2,1)} %get-tuple-element.14) | data formatting | bytes 1835008
  123.2 0.0 copy-done
  123.2 0.9 copy.19
Async XLA Ops:
  0.6 0.7 copy-start.1
  1.3 0.7 copy-start.2
  121.0 2.2 %copy-start = (bf16[896,512]{1,0:T(8,128)(2,1)S(1)}, bf16[896,512]{1,0:T(8,128)(2,1)}, u32[]{:S(2)}) copy-start(bf16[896,512]{1,0:T(8,128)(2,1)} %get-tuple-element.15) | copy-start | bytes 2752516

commit v5 on v4

--- a/solution.py
+++ b/solution.py
@@ -329,11 +329,16 @@
         @pl.when(valid(j - 3))
         def _():
             back_rows(zz_of(j - 3) * 2 + 1 - x)
-            bx_copy(zz_of(j - 3)).start()
 
         return 0
 
     lax.fori_loop(0, 2 * zs + 2, first, 0)
+
+    def start_back(zz, _):
+        bx_copy(zz).start()
+        return 0
+
+    lax.fori_loop(0, zs, start_back, 0)
 
     def slot_forward(b):
         slot_wait(b, across, across)

time: 125 us -> 135 us (1.080)
  Pallas kernels: 115 us -> 125 us
    pallas_call x1, Pallas kernels: 115 us -> 125 us  [one_kernel(): pl.pallas_call(functools.partial(everything, experts, dps), out_shape=(ja...]
where the time goes in v5:
time: 135 us; the launch traced here: 134 us
  Pallas kernels  125 us (93%)
  local copies, waits for them, and re-layouts  8.44 us (6%)
    pallas_call x1, Pallas kernels, one_kernel(): pl.pallas_call(functools.partial(everything, experts, dps), out_shape=(ja...  125 us
    unnamed x11, local copies, waits for them, and re-layouts  6.97 us

profile of v5, /device:TPU:0, one launch (start us, length us, event | category | flops | bytes accessed | tf_op | source)
XLA Modules:
  0.0 134.3 jit_solution(13533364533545915106)
XLA Ops:
  0.6 0.0 copy-start.1
  0.6 0.7 copy-done.1
  1.3 0.0 copy-start.2
  1.3 0.7 copy.11.routes_ref
  2.1 0.0 copy-done.2
  2.1 0.7 copy.12.logits_ref
  2.8 125.2 %shard_map.102 = (bf16[128,896]{1,0:T(8,128)(2,1)}, f32[128,2]{1,0:T(8,128)}, bf16[896,512]{1,0:T(8,128)(2,1)}, bf16[896,512]{1,0:T(8,128)(2,1)}) custom-call(bf16[128,896]{1,0:T(8,128)(2,1)} %tok_ref.1, bf16[128,896]{1,0:T(8,128)(2,1)} %cot_ref.1, s32[128,2]{1,0:T(8,128)} %copy.11.routes_ref, f32[128,2]{1,0:T(8,128)} %copy.12.logits_ref, s32[1,2]{1,0:T(1,128)} %bitcast.1, ...), custom_call_target="tpu_custom_call" | custom-call | tf_op jit(solution)/shard_map/pallas_call | solution.py:470
  128.1 1.5 %copy.13 = f32[128,2]{0,1:T(2,128)} copy(f32[128,2]{1,0:T(8,128)} %get-tuple-element.5) | data formatting | bytes 2048 | tf_op jit(solution)/shard_map/pallas_call | solution.py:470
  129.5 1.6 %copy.17 = bf16[128,896]{1,0:T(8,128)(2,1)} copy(bf16[128,896]{1,0:T(8,128)(2,1)} %get-tuple-element.12) | data formatting | bytes 458752
  131.2 0.0 copy-start
  131.2 2.2 %copy.18 = bf16[896,512]{1,0:T(8,128)(2,1)} copy(bf16[896,512]{1,0:T(8,128)(2,1)} %get-tuple-element.14) | data formatting | bytes 1835008
  133.4 0.0 copy-done
  133.4 0.9 copy.19
Async XLA Ops:
  0.6 0.7 copy-start.1
  1.3 0.7 copy-start.2
  131.2 2.2 %copy-start = (bf16[896,512]{1,0:T(8,128)(2,1)S(1)}, bf16[896,512]{1,0:T(8,128)(2,1)}, u32[]{:S(2)}) copy-start(bf16[896,512]{1,0:T(8,128)(2,1)} %get-tuple-element.15) | copy-start | bytes 2752516
